TPU v7x, 256 devices: a whole 4x4x8 slice. The times are simulated.
256 devices in a mesh: dp: 4 (over y_lo, core), seq: 8 (over y_hi, x), head: 8 (over z).
Axes of the slice: x: 4, y: 4 (y_hi: 2, y_lo: 2; y = y_hi * 2 + y_lo), z: 8, core: 2. Of those that a mesh axis runs over, the one named last changes fastest.
Arguments:
- queries: bfloat16 [4, 2048, 3072], P('dp', 'seq', 'head'), may hold values from -160 to 160
- key_cache: bfloat16 [4, 2048, 1024], P('dp', 'seq', 'head'), may hold values from -7 to 7
- value_cache: bfloat16 [4, 2048, 1024], P('dp', 'seq', 'head'), may hold values from -6 to 6
- out_grad: bfloat16 [4, 2048, 3072], P('dp', 'seq', 'head'), may hold values from -6 to 6
- doc_ids: int32 [4, 2048], P('dp', 'seq'), may hold values from 0 to 1, never falling along the last dimension, each value on 1 to 2047 neighbouring positions
- layer_input: bfloat16 [4, 2048, 3072], P('dp', ('seq', 'head')), may hold values from -6 to 6
- key_proj: bfloat16 [3072, 1024], P(None, 'head'), may hold values from -0.109375 to 0.109375
- value_proj: bfloat16 [3072, 1024], P(None, 'head'), may hold values from -0.109375 to 0.109375
Outputs:
- query_grad: bfloat16 [4, 2048, 3072], P('dp', 'seq', 'head')
- input_grad: bfloat16 [4, 2048, 3072], P('dp', ('seq', 'head'))
- grad_keyproj: float32 [3072, 1024], P(None, 'head')
- grad_valueproj: float32 [3072, 1024], P(None, 'head')
Inputs may be any that keep to these rules, and one draw needn't show every extreme that they name: `doc_ids`: document numbers never fall along a sequence; a document spans 1 to 2047 positions.
All inputs are finite; a program needn't handle non-finite values.
Results may differ from a plain program's by a relative error of at most 0.02.
Values may be sent and summed in bfloat16 or wider, within the bound.
A program may use at most 64 MiB of HBM per device.

v0:
```python
import jax
import jax.numpy as jnp
from jax import lax
from jax.sharding import PartitionSpec as P

D = 3072
HD = 128
GROUP = 3
NEG_FILL = -1e30


def in_order(tiles, dim):
    shape = list(tiles.shape[1:])
    shape[dim] *= tiles.shape[0]
    return jnp.moveaxis(tiles, 0, dim).reshape(shape)


def sent_to_all(x, axis):
    peers = lax.axis_size(axis)
    return lax.all_to_all(jnp.broadcast_to(x[None], (peers, *x.shape)), axis, 0, 0, tiled=True)


def collect(x, axis, dim):
    return in_order(sent_to_all(x, axis), dim)


def in_blocks(x, dim, peers):
    shape = x.shape
    tiles = x.reshape(*shape[:dim], peers, shape[dim] // peers, *shape[dim + 1 :])
    return jnp.moveaxis(tiles, dim, 0)


def sum_at_owner(x, axis, dim):
    tiles = in_blocks(x, dim, lax.axis_size(axis))
    arrived = lax.all_to_all(tiles, axis, split_axis=0, concat_axis=0, tiled=True)
    return arrived.astype(jnp.float32).sum(axis=0)


def shards(queries, key_cache, value_cache, out_grad, doc_ids, layer_input, key_proj, value_proj):
    rows_query = queries.shape[1]
    col_width = key_cache.shape[2]
    kv_heads = col_width // HD
    cycle_size = lax.axis_size("seq")
    head_count = lax.axis_size("head")
    own_index = lax.axis_index("seq")
    score_scale = HD ** (-0.5)
    query_four = queries[0].reshape(rows_query, kv_heads, GROUP, HD)
    grad_four = out_grad[0].reshape(rows_query, kv_heads, GROUP, HD)
    own_blocks = jnp.stack([key_cache[0], value_cache[0]])
    all_docs = collect(doc_ids, "seq", 1)[0]
    query_doc = doc_ids[0]
    query_pos = own_index * rows_query + lax.iota(jnp.int32, rows_query)
    last_pos = own_index * rows_query + rows_query - 1

    def block_scores(kv_piece, row_start):
        row_total = kv_piece.shape[1]
        key_block = kv_piece[0].reshape(row_total, kv_heads, HD)
        value_block = kv_piece[1].reshape(row_total, kv_heads, HD)
        key_pos = row_start + lax.iota(jnp.int32, row_total)
        key_doc = lax.dynamic_slice_in_dim(all_docs, row_start, row_total)
        allowed = (key_pos[None, :] <= query_pos[:, None]) & (
            key_doc[None, :] == query_doc[:, None]
        )
        scores = (
            jnp.einsum("ihge,jhe->hgij", query_four, key_block, preferred_element_type=jnp.float32)
            * score_scale
        )
        masked = jnp.where(allowed, scores, NEG_FILL)
        weight_grad = jnp.einsum(
            "ihge,jhe->hgij", grad_four, value_block, preferred_element_type=jnp.float32
        )
        return (key_block, allowed, masked, weight_grad)

    def stats_block(state_in, kv_piece, row_start):
        row_top, row_sum, row_acc = state_in
        key_block, allowed, masked, weight_grad = block_scores(kv_piece, row_start)
        new_top = jnp.maximum(row_top, jnp.max(masked, axis=-1))
        weights = jnp.where(allowed, jnp.exp(masked - new_top[..., None]), 0.0)
        decay = jnp.exp(row_top - new_top)
        return (
            new_top,
            row_sum * decay + jnp.sum(weights, axis=-1),
            row_acc * decay + jnp.sum(weights * weight_grad, axis=-1),
        )

    def stats_fold(state_in, kv_piece, row_start):
        row_total = kv_piece.shape[1]
        sub_rows = min(row_total, rows_query)

        def one_part(part_num, state_mid):
            part_start = row_start + part_num * sub_rows
            sub_piece = kv_piece
            return lax.cond(
                part_start <= last_pos,
                lambda: stats_block(state_mid, sub_piece, part_start),
                lambda: state_mid,
            )

        return lax.fori_loop(0, row_total // sub_rows, one_part, state_in)

    stat_shape = (kv_heads, GROUP, rows_query)
    stats_init = (
        jnp.full(stat_shape, NEG_FILL, jnp.float32),
        jnp.zeros(stat_shape, jnp.float32),
        jnp.zeros(stat_shape, jnp.float32),
    )
    all_blocks = collect(own_blocks, "seq", 1)
    row_top, row_sum, row_acc = lax.fori_loop(
        0,
        cycle_size,
        lambda block_num, state_mid: stats_fold(
            state_mid,
            lax.dynamic_slice_in_dim(all_blocks, block_num * rows_query, rows_query, 1),
            block_num * rows_query,
        ),
        stats_init,
    )
    log_total = row_top + jnp.log(row_sum)
    row_delta = row_acc / row_sum

    def grad_block(kv_piece, row_start):
        row_total = kv_piece.shape[1]
        key_block, allowed, masked, weight_grad = block_scores(kv_piece, row_start)
        weights = jnp.where(allowed, jnp.exp(masked - log_total[..., None]), 0.0)
        score_grad = (weights * (weight_grad - row_delta[..., None]) * score_scale).astype(
            jnp.bfloat16
        )
        weights_low = weights.astype(jnp.bfloat16)
        query_add = jnp.einsum(
            "hgij,jhe->ihge", score_grad, key_block, preferred_element_type=jnp.float32
        )
        key_add = jnp.einsum(
            "hgij,ihge->jhe", score_grad, query_four, preferred_element_type=jnp.float32
        )
        value_add = jnp.einsum(
            "hgij,ihge->jhe", weights_low, grad_four, preferred_element_type=jnp.float32
        )
        return (
            query_add,
            jnp.stack(
                [key_add.reshape(row_total, col_width), value_add.reshape(row_total, col_width)]
            ),
        )

    zero_query = jnp.zeros((rows_query, kv_heads, GROUP, HD), jnp.float32)

    def guarded(kv_piece, row_start):
        return lax.cond(
            row_start <= last_pos,
            lambda: grad_block(kv_piece, row_start),
            lambda: (zero_query, jnp.zeros(kv_piece.shape, jnp.float32)),
        )

    def gathered_turn(block_num, state_mid):
        grad_terms, query_sum = state_mid
        row_start = block_num * rows_query
        kv_piece = lax.dynamic_slice_in_dim(all_blocks, row_start, rows_query, 1)
        query_add, kv_add = guarded(kv_piece, row_start)
        return (
            lax.dynamic_update_slice_in_dim(grad_terms, kv_add, row_start, 1),
            query_sum + query_add,
        )

    terms_init = jnp.zeros(all_blocks.shape, jnp.float32)
    grad_terms, query_sum = lax.fori_loop(0, cycle_size, gathered_turn, (terms_init, zero_query))
    kv_grads = sum_at_owner(grad_terms.astype(jnp.bfloat16), "seq", 1)
    query_grad = query_sum.astype(jnp.bfloat16).reshape(1, rows_query, kv_heads * GROUP * HD)
    kv_low = kv_grads.astype(jnp.bfloat16)
    input_rows = rows_query // head_count
    contract_cols = (((1,), (1,)), ((), ()))
    sub_grads = kv_low
    key_term = lax.dot_general(
        sub_grads[0], key_proj, contract_cols, preferred_element_type=jnp.float32
    )
    value_term = lax.dot_general(
        sub_grads[1], value_proj, contract_cols, preferred_element_type=jnp.float32
    )
    input_sum = lax.psum_scatter(
        (key_term + value_term).astype(jnp.bfloat16), "head", scatter_dimension=0, tiled=True
    )
    input_grad = input_sum.reshape(1, input_rows, D)
    contract_rows = (((0,), (0,)), ((), ()))
    input_piece = collect(layer_input[0], "head", 0)
    row_total = input_piece.shape[0]
    sub_grads = kv_low
    key_part = lax.dot_general(
        input_piece, sub_grads[0], contract_rows, preferred_element_type=jnp.float32
    )
    value_part = lax.dot_general(
        input_piece, sub_grads[1], contract_rows, preferred_element_type=jnp.float32
    )
    grad_keyproj, grad_valueproj = (
        lax.psum(key_part.astype(jnp.bfloat16), ("dp", "seq")).astype(jnp.float32),
        lax.psum(value_part.astype(jnp.bfloat16), ("dp", "seq")).astype(jnp.float32),
    )
    return (query_grad, input_grad, grad_keyproj, grad_valueproj)


def solution(mesh):
    return jax.shard_map(
        shards,
        mesh=mesh,
        in_specs=(
            P("dp", "seq", "head"),
            P("dp", "seq", "head"),
            P("dp", "seq", "head"),
            P("dp", "seq", "head"),
            P("dp", "seq"),
            P("dp", ("seq", "head"), None),
            P(None, "head"),
            P(None, "head"),
        ),
        out_specs=(
            P("dp", "seq", "head"),
            P("dp", ("seq", "head"), None),
            P(None, "head"),
            P(None, "head"),
        ),
        check_vma=False,
    )
```

profile of v0, /device:TPU:6, one launch (start us, length us, event | category | flops | bytes accessed | tf_op | source)
XLA Modules:
  0.0 297.8 jit_solution(2051672772160471777)
XLA Ops:
  8.0 1.0 pad_maximum_fusion.1
  9.2 22.5 %all_to_all.20 = bf16[8,2,256,128]{3,2,1,0:T(8,128)(2,1)S(1)} all-to-all(bf16[8,2,256,128]{3,2,1,0:T(8,128)(2,1)S(1)} %broadcast_in_dim.75), channel_id=1, replica_groups=mesh['dp'=4,'seq'=8,'head'=8] {'seq'}, dimensions={0} | all-to-all | bytes 2097152 | tf_op jit(solution)/shard_map/all_to_all | solution.py:20
  32.3 5.3 %all-to-all-start.1 = ((s32[8,1,256]{2,1,0:T(1,128)}), s32[8,1,256]{2,1,0:T(1,128)S(1)}, u32[]{:S(2)}, u32[]{:S(2)}) async-start(s32[8,1,256]{2,1,0:T(1,128)} %broadcast_in_dim.77), calls=%async_computation.1 | async-start | bytes 16384 | tf_op jit(solution)/shard_map/all_to_all | solution.py:20
  38.3 1.0 copy.41
  39.3 4.0 %all-to-all-done.1 = s32[8,1,256]{2,1,0:T(1,128)S(1)} async-done(((s32[8,1,256]{2,1,0:T(1,128)}), s32[8,1,256]{2,1,0:T(1,128)S(1)}, u32[]{:S(2)}, u32[]{:S(2)}) %all-to-all-start.1) | async-done | bytes 8224 | tf_op jit(solution)/shard_map/all_to_all | solution.py:20
  43.3 11.4 %while.49 = (s32[]{:T(128)}, f32[1,3,256]{2,1,0:T(4,128)S(1)}, f32[1,3,256]{2,1,0:T(4,128)S(1)}, f32[1,3,256]{2,1,0:T(4,128)S(1)}, s32[]{:T(128)}, /*index=5*/s3...) while((s32[]{:T(128)}, f32[1,3,256]{2,1,0:T(4,128)S(1)}, ...), condition=%wide.region_6.7_spmd.clone, body=%wide.region_0.6_spmd.clone.sunk | while | flops 102828800 | bytes 3211637 | solution.py:108
  43.3 2.8 conditional.6
  43.5 1.1 fusion.36
  44.7 1.2 fusion.7
  46.1 2.8 conditional.6
  46.3 1.1 fusion.36
  47.5 1.2 fusion.7
  48.9 2.8 conditional.6
  49.2 1.1 fusion.36
  50.3 1.2 fusion.7
  51.7 2.8 conditional.6
  52.0 1.1 fusion.36
  53.1 1.2 fusion.7
  54.7 1.0 broadcast_in_dim.73
  55.8 23.7 %while.50 = (s32[]{:T(128)}, bf16[2,2048,128]{2,1,0:T(8,128)(2,1)}, f32[256,1,3,128]{0,3,2,1:T(8,128)S(1)}, s32[]{:T(128)}, bf16[2,2048,128]{2,1,0:T(8,128)(2,1)...) while((s32[]{:T(128)}, bf16[2,2048,128]{2,1,0:T(8,128)(2,1)}, ...), condition=%wide.region_10.0_spmd.clone, body=%wide.region_7.10_spmd.clone.sunk | while | flops 253886976 | bytes 6900105 | solution.py:165
  55.8 4.2 %conditional.7 = (f32[256,1,3,128]{0,3,2,1:T(8,128)S(1)}, bf16[2,256,128]{2,1,0:T(8,128)(2,1)S(1)}) conditional(s32[]{:T(128)} %convert_element_type.80, () %tuple.114, (bf16[2,2048,128]{2,1,0:T(8,128)(2,1)}, s32[]{:T(128)}, s32[]{:T(128)}, s32[]{:T(128)}, s32[2048]{0:T(1024)S(1)}, /*index=5*/s32[1,256]{1,0:T(1,128)S(1)}, ...), branch_computations={%region_8.8_spmd, %region_9.9_spmd} | conditional | flops 253690368 | bytes 5456462 | solution.py:148
  56.0 1.2 fusion.21
  57.2 1.1 fusion.22
  58.3 1.1 convolution_bitcast_fusion.2
  60.8 4.2 %conditional.7 = (f32[256,1,3,128]{0,3,2,1:T(8,128)S(1)}, bf16[2,256,128]{2,1,0:T(8,128)(2,1)S(1)}) conditional(s32[]{:T(128)} %convert_element_type.80, () %tuple.114, (bf16[2,2048,128]{2,1,0:T(8,128)(2,1)}, s32[]{:T(128)}, s32[]{:T(128)}, s32[]{:T(128)}, s32[2048]{0:T(1024)S(1)}, /*index=5*/s32[1,256]{1,0:T(1,128)S(1)}, ...), branch_computations={%region_8.8_spmd, %region_9.9_spmd} | conditional | flops 253690368 | bytes 5456462 | solution.py:148
  61.0 1.2 fusion.21
  62.2 1.1 fusion.22
  63.3 1.1 convolution_bitcast_fusion.2
  65.8 4.2 %conditional.7 = (f32[256,1,3,128]{0,3,2,1:T(8,128)S(1)}, bf16[2,256,128]{2,1,0:T(8,128)(2,1)S(1)}) conditional(s32[]{:T(128)} %convert_element_type.80, () %tuple.114, (bf16[2,2048,128]{2,1,0:T(8,128)(2,1)}, s32[]{:T(128)}, s32[]{:T(128)}, s32[]{:T(128)}, s32[2048]{0:T(1024)S(1)}, /*index=5*/s32[1,256]{1,0:T(1,128)S(1)}, ...), branch_computations={%region_8.8_spmd, %region_9.9_spmd} | conditional | flops 253690368 | bytes 5456462 | solution.py:148
  66.0 1.2 fusion.21
  67.3 1.1 fusion.22
  68.4 1.1 convolution_bitcast_fusion.2
  70.8 4.2 %conditional.7 = (f32[256,1,3,128]{0,3,2,1:T(8,128)S(1)}, bf16[2,256,128]{2,1,0:T(8,128)(2,1)S(1)}) conditional(s32[]{:T(128)} %convert_element_type.80, () %tuple.114, (bf16[2,2048,128]{2,1,0:T(8,128)(2,1)}, s32[]{:T(128)}, s32[]{:T(128)}, s32[]{:T(128)}, s32[2048]{0:T(1024)S(1)}, /*index=5*/s32[1,256]{1,0:T(1,128)S(1)}, ...), branch_computations={%region_8.8_spmd, %region_9.9_spmd} | conditional | flops 253690368 | bytes 5456462 | solution.py:148
  71.1 1.2 fusion.21
  72.3 1.1 fusion.22
  73.4 1.1 convolution_bitcast_fusion.2
  79.4 1.3 copy.48
  80.8 44.8 %all_to_all.21 = bf16[8,2,256,128]{3,2,1,0:T(8,128)(2,1)} all-to-all(bf16[8,2,256,128]{3,2,1,0:T(8,128)(2,1)S(1)} %copy.48), channel_id=1, replica_groups=mesh['dp'=4,'seq'=8,'head'=8] {'seq'}, dimensions={0} | all-to-all | bytes 2097152 | tf_op jit(solution)/shard_map/all_to_all | solution.py:35
  125.5 1.3 broadcast_in_dim.80
  126.8 8.5 %all-to-all-start.3 = ((bf16[8,32,3072]{2,1,0:T(8,128)(2,1)}), bf16[8,32,3072]{2,1,0:T(8,128)(2,1)S(1)}, u32[]{:S(2)}, u32[]{:S(2)}) async-start(bf16[8,32,3072]{2,1,0:T(8,128)(2,1)} %broadcast_in_dim.80), calls=%async_computation.4 | async-start | bytes 3145728 | tf_op jit(solution)/shard_map/all_to_all | solution.py:20
  135.3 1.4 reduce_sum.34
  136.7 34.5 %all-to-all-done.3 = bf16[8,32,3072]{2,1,0:T(8,128)(2,1)S(1)} async-done(((bf16[8,32,3072]{2,1,0:T(8,128)(2,1)}), bf16[8,32,3072]{2,1,0:T(8,128)(2,1)S(1)}, u32[]{:S(2)}, u32[]{:S(2)}) %all-to-all-start.3) | async-done | bytes 1572896 | tf_op jit(solution)/shard_map/all_to_all | solution.py:20
  171.2 1.3 fusion.33
  172.5 1.3 fusion.34
  174.9 1.7 fusion.32
  177.5 108.8 %all-reduce.3.cloned.1.call-done = (bf16[3072,128]{0,1:T(8,128)(2,1)}, bf16[3072,128]{0,1:T(8,128)(2,1)}) async-done(((bf16[3072,128]{0,1:T(8,128)(2,1)}, bf16[3072,128]{0,1:T(8,128)(2,1)}), (bf16[3072,128]{0,1:T(8,128)(2,1)}, bf16[3072,128]{0,1:T(8,128)(2,1)})) %all-reduce.3.cloned.1.call-update) | async-done | bytes 1572880 | tf_op jit(solution)/shard_map/psum | solution.py:193
  286.4 2.6 copy.50
  289.0 1.4 copy.51
  (133 shorter events, 14.9 us)
Async XLA Ops:
  8.0 165.8 %copy-start = (bf16[3072,128]{1,0:T(8,128)(2,1)S(1)}, bf16[3072,128]{1,0:T(8,128)(2,1)}, u32[]{:S(2)}) copy-start(bf16[3072,128]{1,0:T(8,128)(2,1)} %param.22) | copy-start | bytes 2359300
  9.0 22.7 %copy-start.6 = (s32[1,256]{1,0:T(1,128)S(1)}, s32[1,256]{1,0:T(1,128)}, u32[]{:S(2)}) copy-start(s32[1,256]{1,0:T(1,128)} %param.20) | copy-start | bytes 3076
  9.0 28.6 %copy-start.4 = (bf16[1,256,384]{2,1,0:T(8,128)(2,1)S(1)}, bf16[1,256,384]{2,1,0:T(8,128)(2,1)}, u32[]{:S(2)}) copy-start(bf16[1,256,384]{2,1,0:T(8,128)(2,1)} %param.16) | copy-start | bytes 589828
  9.2 28.7 %copy-start.5 = (bf16[1,256,384]{2,1,0:T(8,128)(2,1)S(1)}, bf16[1,256,384]{2,1,0:T(8,128)(2,1)}, u32[]{:S(2)}) copy-start(bf16[1,256,384]{2,1,0:T(8,128)(2,1)} %param.19) | copy-start | bytes 589828
  32.3 10.9 %all-to-all-start.1 = ((s32[8,1,256]{2,1,0:T(1,128)}), s32[8,1,256]{2,1,0:T(1,128)S(1)}, u32[]{:S(2)}, u32[]{:S(2)}) async-start(s32[8,1,256]{2,1,0:T(1,128)} %broadcast_in_dim.77), calls=%async_computation.1 | async-start | bytes 16384 | tf_op jit(solution)/shard_map/all_to_all | solution.py:20
  80.7 44.8 %copy-start.3 = (bf16[1,32,3072]{2,1,0:T(8,128)(2,1)S(1)}, bf16[1,32,3072]{2,1,0:T(8,128)(2,1)}, u32[]{:S(2)}) copy-start(bf16[1,32,3072]{2,1,0:T(8,128)(2,1)} %param.21) | copy-start | bytes 589828
  126.8 44.3 %all-to-all-start.3 = ((bf16[8,32,3072]{2,1,0:T(8,128)(2,1)}), bf16[8,32,3072]{2,1,0:T(8,128)(2,1)S(1)}, u32[]{:S(2)}, u32[]{:S(2)}) async-start(bf16[8,32,3072]{2,1,0:T(8,128)(2,1)} %broadcast_in_dim.80), calls=%async_computation.4 | async-start | bytes 3145728 | tf_op jit(solution)/shard_map/all_to_all | solution.py:20
  135.3 151.1 %all-reduce.3.cloned.1.call-start = ((), (), s32[]{:S(2)}) async-start(), calls=%async_computation.6 | async-start | bytes 3145728 | tf_op jit(solution)/shard_map/psum | solution.py:193
  173.8 1.1 copy-start.2
  173.8 116.6 %reduce-scatter.2.cloned.1.call-start = ((), (), s32[]{:S(2)}) async-start(), calls=%async_computation.5 | async-start | bytes 1769472 | tf_op jit(solution)/shard_map/reduce_scatter | solution.py:178
  286.4 2.6 copy-start.1
Sparse Core Ops, SparseCore 0:
  173.9 112.4 all-reduce.2
Sparse Core Ops, SparseCore 1:
  177.4 34.9 reduce-scatter.1
where the time goes:
time: 300 us; the launch traced here: 298 us
  waiting for transfers between devices  147 us (49%)
  blocking collectives  67.3 us (22%)
  matrix products  29.5 us (10%)
  local copies, waits for them, and re-layouts  17.7 us (6%)
  between operations  15.6 us (5%)
  starting transfers between devices  13.8 us (5%)
  other arithmetic  5.27 us (2%)
    psum x1, waiting for transfers between devices, shards(): lax.psum(key_part.astype(jnp.bfloat16), ('dp', 'seq')).astype(jnp.float32)  109 us
    all_to_all x1, blocking collectives, sum_at_owner(): lax.all_to_all(tiles, axis, split_axis=0, concat_axis=0, tiled=True)  44.8 us
    all_to_all x2, waiting for transfers between devices, sent_to_all(): lax.all_to_all(jnp.broadcast_to(x[None], (peers, *x.shape)), axis, 0, 0,...  38.4 us
    all_to_all x1, blocking collectives, sent_to_all(): lax.all_to_all(jnp.broadcast_to(x[None], (peers, *x.shape)), axis, 0, 0,...  22.5 us
    all_to_all x2, starting transfers between devices, sent_to_all(): lax.all_to_all(jnp.broadcast_to(x[None], (peers, *x.shape)), axis, 0, 0,...  13.8 us
    dot_general x8, matrix products, block_scores(): jnp.einsum('ihge,jhe->hgij', query_four, key_block, preferred_element_typ...  9.29 us
    dot_general x8, matrix products, block_scores(): jnp.einsum('ihge,jhe->hgij', grad_four, value_block, preferred_element_ty...  9.06 us
  transfers between devices with their start and end apart: 4, of which 3 were waited for; matrix products, arithmetic and copies ran while one was open for 3% of the time, Pallas kernels for 0%

commit v1 on v0

--- a/solution.py
+++ b/solution.py
@@ -190,7 +190,9 @@
         input_piece, sub_grads[1], contract_rows, preferred_element_type=jnp.float32
     )
     grad_keyproj, grad_valueproj = (
-        lax.psum(key_part.astype(jnp.bfloat16), ("dp", "seq")).astype(jnp.float32),
+        jnp.sum(lax.all_gather(key_part.astype(jnp.bfloat16), ("dp", "seq")), axis=0).astype(
+            jnp.float32
+        ),
         lax.psum(value_part.astype(jnp.bfloat16), ("dp", "seq")).astype(jnp.float32),
     )
     return (query_grad, input_grad, grad_keyproj, grad_valueproj)

time: 300 us -> 467 us (1.56)
  waiting for transfers between devices: 147 us -> 287 us
  local copies, waits for them, and re-layouts: 17.7 us -> 33 us
  other arithmetic: 5.27 us -> 14.5 us
    all_gather x0 -> x1, waiting for transfers between devices: none -> 144 us  [shards(): lax.all_gather(key_part.astype(jnp.bfloat16), ('dp', 'seq'))]
    unnamed x21 -> x22, local copies, waits for them, and re-layouts: 5.99 us -> 28.7 us
    reduce_sum x0 -> x1, other arithmetic: none -> 9.23 us  [shards(): jnp.sum(lax.all_gather(key_part.astype(jnp.bfloat16), ('dp', 'seq')), axi...]
    dynamic_update_slice x8, local copies, waits for them, and re-layouts: 5.37 us -> 0.21 us  [gathered_turn(): lax.dynamic_update_slice_in_dim(grad_terms, kv_add, row_start, 1)]
  transfers between devices with their start and end apart: 4 -> 5, of which waited for: 3 -> 4; matrix products, arithmetic and copies ran while one was open for 3% -> 9% of each run, Pallas kernels for 0% -> 0%
where the time goes in v1:
time: 467 us; the launch traced here: 463 us
  waiting for transfers between devices  287 us (61%)
  blocking collectives  67.4 us (14%)
  local copies, waits for them, and re-layouts  33 us (7%)
  matrix products  29.6 us (6%)
  between operations  15.7 us (3%)
  other arithmetic  14.5 us (3%)
  starting transfers between devices  13.9 us (3%)
    all_gather x1, waiting for transfers between devices, shards(): lax.all_gather(key_part.astype(jnp.bfloat16), ('dp', 'seq'))  144 us
    psum x1, waiting for transfers between devices, shards(): lax.psum(value_part.astype(jnp.bfloat16), ('dp', 'seq')).astype(jnp.float32)  105 us
    all_to_all x1, blocking collectives, sum_at_owner(): lax.all_to_all(tiles, axis, split_axis=0, concat_axis=0, tiled=True)  44.9 us
    all_to_all x2, waiting for transfers between devices, sent_to_all(): lax.all_to_all(jnp.broadcast_to(x[None], (peers, *x.shape)), axis, 0, 0,...  38.4 us
    unnamed x22, local copies, waits for them, and re-layouts  28.7 us
    all_to_all x1, blocking collectives, sent_to_all(): lax.all_to_all(jnp.broadcast_to(x[None], (peers, *x.shape)), axis, 0, 0,...  22.5 us
    all_to_all x2, starting transfers between devices, sent_to_all(): lax.all_to_all(jnp.broadcast_to(x[None], (peers, *x.shape)), axis, 0, 0,...  13.7 us
  transfers between devices with their start and end apart: 5, of which 4 were waited for; matrix products, arithmetic and copies ran while one was open for 9% of the time, Pallas kernels for 0%

profile of v1, /device:TPU:6, one launch (start us, length us, event | category | flops | bytes accessed | tf_op | source)
XLA Modules:
  0.0 463.1 jit_solution(11708358642509857053)
XLA Ops:
  9.2 22.5 %all_to_all.20 = bf16[8,2,256,128]{3,2,1,0:T(8,128)(2,1)S(1)} all-to-all(bf16[8,2,256,128]{3,2,1,0:T(8,128)(2,1)S(1)} %broadcast_in_dim.75), channel_id=1, replica_groups=mesh['dp'=4,'seq'=8,'head'=8] {'seq'}, dimensions={0} | all-to-all | bytes 2097152 | tf_op jit(solution)/shard_map/all_to_all | solution.py:20
  32.3 5.3 %all-to-all-start.1 = ((s32[8,1,256]{2,1,0:T(1,128)}), s32[8,1,256]{2,1,0:T(1,128)S(1)}, u32[]{:S(2)}, u32[]{:S(2)}) async-start(s32[8,1,256]{2,1,0:T(1,128)} %broadcast_in_dim.77), calls=%async_computation.1 | async-start | bytes 16384 | tf_op jit(solution)/shard_map/all_to_all | solution.py:20
  38.3 1.0 copy.39
  39.3 4.0 all-to-all-done.1
  43.3 11.5 %while.49 = (s32[]{:T(128)}, f32[1,3,256]{2,1,0:T(4,128)S(1)}, f32[1,3,256]{2,1,0:T(4,128)S(1)}, f32[1,3,256]{2,1,0:T(4,128)S(1)}, s32[]{:T(128)}, /*index=5*/s3...) while((s32[]{:T(128)}, f32[1,3,256]{2,1,0:T(4,128)S(1)}, ...), condition=%wide.region_6.7_spmd.clone, body=%wide.region_0.6_spmd.clone.sunk | while | flops 102828800 | bytes 3211629 | solution.py:108
  43.3 2.8 conditional.6
  43.5 1.1 fusion.36
  44.7 1.2 fusion.7
  46.1 2.8 conditional.6
  46.4 1.1 fusion.36
  47.5 1.2 fusion.7
  48.9 2.8 conditional.6
  49.2 1.1 fusion.36
  50.3 1.2 fusion.7
  51.7 2.8 conditional.6
  52.0 1.1 fusion.36
  53.1 1.2 fusion.7
  54.8 18.8 %while.50 = (s32[]{:T(128)}, bf16[2,2048,128]{2,1,0:T(8,128)(2,1)S(1)}, f32[256,1,3,128]{0,3,2,1:T(8,128)S(1)}, s32[]{:T(128)}, bf16[2,2048,128]{2,1,0:T(8,128)(...) while((s32[]{:T(128)}, ...), condition=%wide.region_10.0_spmd.clone, body=%wide.region_7.10_spmd.clone.sunk | while | flops 253886976 | bytes 6899597 | solution.py:165
  54.9 4.2 conditional.7
  55.1 1.2 fusion.21
  56.6 1.1 fusion.22
  57.7 1.1 convolution_bitcast_fusion.2
  59.3 4.2 conditional.7
  59.6 1.2 fusion.21
  61.0 1.1 fusion.22
  62.1 1.1 convolution_bitcast_fusion.2
  63.7 4.2 conditional.7
  64.0 1.2 fusion.21
  65.4 1.1 fusion.22
  66.6 1.1 convolution_bitcast_fusion.2
  68.1 4.2 conditional.7
  68.4 1.2 fusion.21
  69.8 1.1 fusion.22
  71.0 1.1 convolution_bitcast_fusion.2
  73.7 44.9 %all_to_all.21 = bf16[8,2,256,128]{3,2,1,0:T(8,128)(2,1)} all-to-all(bf16[8,2,256,128]{3,2,1,0:T(8,128)(2,1)S(1)} %copy.46), channel_id=1, replica_groups=mesh['dp'=4,'seq'=8,'head'=8] {'seq'}, dimensions={0} | all-to-all | bytes 2097152 | tf_op jit(solution)/shard_map/all_to_all | solution.py:35
  118.6 1.3 broadcast_in_dim.80
  119.9 8.5 %all-to-all-start.3 = ((bf16[8,32,3072]{2,1,0:T(8,128)(2,1)}), bf16[8,32,3072]{2,1,0:T(8,128)(2,1)S(1)}, u32[]{:S(2)}, u32[]{:S(2)}) async-start(bf16[8,32,3072]{2,1,0:T(8,128)(2,1)} %broadcast_in_dim.80), calls=%async_computation.4 | async-start | bytes 3145728 | tf_op jit(solution)/shard_map/all_to_all | solution.py:20
  128.4 1.4 reduce_sum.46
  129.8 34.4 %all-to-all-done.3 = bf16[8,32,3072]{2,1,0:T(8,128)(2,1)S(1)} async-done(((bf16[8,32,3072]{2,1,0:T(8,128)(2,1)}), bf16[8,32,3072]{2,1,0:T(8,128)(2,1)S(1)}, u32[]{:S(2)}, u32[]{:S(2)}) %all-to-all-start.3) | async-done | bytes 1572896 | tf_op jit(solution)/shard_map/all_to_all | solution.py:20
  164.2 1.3 fusion.34
  165.6 1.3 fusion.33
  168.0 1.8 fusion.32
  170.7 105.3 %all-reduce.2.cloned.1.call-done = bf16[3072,128]{0,1:T(8,128)(2,1)} async-done(((bf16[3072,128]{0,1:T(8,128)(2,1)}), bf16[3072,128]{0,1:T(8,128)(2,1)}) %all-reduce.2.cloned.1.call-update) | async-done | bytes 786448 | tf_op jit(solution)/shard_map/psum | solution.py:196
  276.0 2.5 copy.49
  278.5 143.7 %all-gather.3.cloned.1.call-done = bf16[98304,128]{0,1:T(8,128)(2,1)} async-done(((bf16[3072,128]{0,1:T(8,128)(2,1)}), bf16[98304,128]{0,1:T(8,128)(2,1)}) %all-gather.3.cloned.1.call-update) | async-done | bytes 25165840 | tf_op jit(solution)/shard_map/all_gather | solution.py:193
  422.3 22.7 %copy.53 = bf16[16,8,32,3072]{3,2,1,0:T(8,128)(2,1)S(1)} copy(bf16[16,8,32,3072]{3,1,2,0:T(8,128)(2,1)} %bitcast.156) | data formatting | bytes 50331648
  445.0 9.2 %bitcast_reduce_fusion = bf16[3072,128]{0,1:T(8,128)(2,1)S(1)} fusion(bf16[16,8,32,3072]{3,2,1,0:T(8,128)(2,1)S(1)} %copy.53), kind=kLoop, calls=%fused_computation.55 | loop fusion | flops 12189696 | bytes 25952256 | tf_op jit(solution)/shard_map/reduce_sum | solution.py:193
  454.3 1.4 copy.48
  (138 shorter events, 11.0 us)
Async XLA Ops:
  8.0 159.0 %copy-start = (bf16[3072,128]{1,0:T(8,128)(2,1)S(1)}, bf16[3072,128]{1,0:T(8,128)(2,1)}, u32[]{:S(2)}) copy-start(bf16[3072,128]{1,0:T(8,128)(2,1)} %param.22) | copy-start | bytes 2359300
  9.0 22.7 %copy-start.6 = (s32[1,256]{1,0:T(1,128)S(1)}, s32[1,256]{1,0:T(1,128)}, u32[]{:S(2)}) copy-start(s32[1,256]{1,0:T(1,128)} %param.20) | copy-start | bytes 3076
  9.0 28.6 %copy-start.4 = (bf16[1,256,384]{2,1,0:T(8,128)(2,1)S(1)}, bf16[1,256,384]{2,1,0:T(8,128)(2,1)}, u32[]{:S(2)}) copy-start(bf16[1,256,384]{2,1,0:T(8,128)(2,1)} %param.16) | copy-start | bytes 589828
  9.2 28.7 %copy-start.5 = (bf16[1,256,384]{2,1,0:T(8,128)(2,1)S(1)}, bf16[1,256,384]{2,1,0:T(8,128)(2,1)}, u32[]{:S(2)}) copy-start(bf16[1,256,384]{2,1,0:T(8,128)(2,1)} %param.19) | copy-start | bytes 589828
  32.3 10.9 %all-to-all-start.1 = ((s32[8,1,256]{2,1,0:T(1,128)}), s32[8,1,256]{2,1,0:T(1,128)S(1)}, u32[]{:S(2)}, u32[]{:S(2)}) async-start(s32[8,1,256]{2,1,0:T(1,128)} %broadcast_in_dim.77), calls=%async_computation.1 | async-start | bytes 16384 | tf_op jit(solution)/shard_map/all_to_all | solution.py:20
  73.7 44.9 %copy-start.3 = (bf16[1,32,3072]{2,1,0:T(8,128)(2,1)S(1)}, bf16[1,32,3072]{2,1,0:T(8,128)(2,1)}, u32[]{:S(2)}) copy-start(bf16[1,32,3072]{2,1,0:T(8,128)(2,1)} %param.21) | copy-start | bytes 589828
  119.9 44.3 %all-to-all-start.3 = ((bf16[8,32,3072]{2,1,0:T(8,128)(2,1)}), bf16[8,32,3072]{2,1,0:T(8,128)(2,1)S(1)}, u32[]{:S(2)}, u32[]{:S(2)}) async-start(bf16[8,32,3072]{2,1,0:T(8,128)(2,1)} %broadcast_in_dim.80), calls=%async_computation.4 | async-start | bytes 3145728 | tf_op jit(solution)/shard_map/all_to_all | solution.py:20
  128.4 147.6 %all-reduce.2.cloned.1.call-start = ((), (), s32[]{:S(2)}) async-start(), calls=%async_computation.6 | async-start | bytes 1572864 | tf_op jit(solution)/shard_map/psum | solution.py:196
  165.5 256.7 %all-gather.3.cloned.1.call-start = ((), (), s32[]{:S(2)}) async-start(), calls=%async_computation.7 | async-start | bytes 25952256 | tf_op jit(solution)/shard_map/all_gather | solution.py:193
  166.9 1.1 copy-start.2
  166.9 288.8 %reduce-scatter.2.cloned.1.call-start = ((), (), s32[]{:S(2)}) async-start(), calls=%async_computation.5 | async-start | bytes 1769472 | tf_op jit(solution)/shard_map/reduce_scatter | solution.py:178
  445.0 10.7 %copy-start.1 = (bf16[3072,128]{1,0:T(8,128)(2,1)S(1)}, bf16[3072,128]{1,0:T(8,128)(2,1)}, u32[]{:S(2)}) copy-start(bf16[3072,128]{1,0:T(8,128)(2,1)} %param.22) | copy-start | bytes 2359300
Sparse Core Ops, SparseCore 0:
  165.7 110.2 all-reduce.1
  278.4 143.8 all-gather.2
Sparse Core Ops, SparseCore 1:
  170.5 34.6 reduce-scatter.1
